TPU v7x, 32 devices: a whole 2x2x4 slice. The times are simulated.
32 devices in a mesh: row: 4 (over y, x), col: 8 (over z, core).
Axes of the slice: x: 2, y: 2, z: 4, core: 2. Of those that a mesh axis runs over, the one named last changes fastest.
Arguments:
- fingerprints: bfloat16 [8192, 1024], P(('row', 'col')), as said below
- probes: bfloat16 [8192, 256], P(('row', 'col')), may hold values from -6 to 6
Outputs:
- image: float32 [8192, 256], P(('row', 'col'))
Inputs may be any that keep to these rules, and one draw needn't show every extreme that they name: `fingerprints`: every entry is positive.
All inputs are finite; a program needn't handle non-finite values.
Results may differ from a plain program's by a relative error of at most 0.0031.
Values may be sent and summed in bfloat16 or wider, within the bound.
A program may use at most 64 MiB of HBM per device.

v0:
```python
import math
import jax
import jax.numpy as jnp
from jax import lax
from jax.sharding import PartitionSpec as P


def squares(rows_now):
    values = rows_now.astype(jnp.float32)
    return jnp.sum(values * values, axis=1)


def tanimoto(first_rows, second_rows, first_sq, second_sq):
    inner = lax.dot_general(
        first_rows, second_rows, (((1,), (1,)), ((), ())), preferred_element_type=jnp.float32
    )
    kernel = inner / (first_sq[:, None] + second_sq[None, :] - inner)
    return kernel.astype(jnp.bfloat16)


def per_device(fingerprints, probes):
    molecules = fingerprints.shape[0] * lax.axis_size("row") * lax.axis_size("col")
    factor = 1.0 / math.sqrt(molecules)
    column_rows, column_probes = (
        lax.all_gather(fingerprints, "row", axis=0, tiled=True),
        lax.all_gather(probes, "row", axis=0, tiled=True),
    )
    column_sq = squares(column_rows)
    shard_rows = lax.all_gather(fingerprints, "col", axis=0, tiled=True)
    kernel = tanimoto(shard_rows, column_rows, squares(shard_rows), column_sq)
    partial_value = jnp.dot(kernel, column_probes, preferred_element_type=jnp.float32)
    owned = lax.psum_scatter(partial_value, "col", scatter_dimension=0, tiled=True)
    return owned * factor


def solution(mesh):
    return jax.shard_map(
        per_device,
        mesh=mesh,
        in_specs=(P(("row", "col"), None), P(("row", "col"), None)),
        out_specs=P(("row", "col"), None),
        check_vma=False,
    )
```

profile of v0, /device:TPU:0, one launch (start us, length us, event | category | flops | bytes accessed | tf_op | source)
XLA Modules:
  0.0 151.5 jit_solution(15270870452908466009)
XLA Ops:
  6.5 0.0 all-gather.5.cloned.1.call-start
  6.5 0.7 all-gather.5.cloned.1.call-update
  7.3 0.0 all-gather.3.cloned.1.call-start
  7.3 0.7 all-gather.3.cloned.1.call-update
  8.0 0.0 reduce-scatter.2.cloned.1.call-start
  8.1 11.8 %all_gather.11 = bf16[1024,256]{1,0:T(8,128)(2,1)S(1)} all-gather(bf16[256,256]{1,0:T(8,128)(2,1)} %param.3), channel_id=1, replica_groups=mesh['row'=4,'col'=8] {'row'}, dimensions={0}, use_global_device_ids=true | all-gather | bytes 655360 | tf_op jit(solution)/shard_map/all_gather | solution.py:26
  19.9 27.4 %all-gather.5.cloned.1.call-done = bf16[1024,1024]{1,0:T(8,128)(2,1)} async-done(((bf16[256,1024]{1,0:T(8,128)(2,1)}), bf16[1024,1024]{1,0:T(8,128)(2,1)}) %all-gather.5.cloned.1.call-update) | async-done | bytes 2097168 | tf_op jit(solution)/shard_map/all_gather | solution.py:25
  47.2 0.0 copy-start
  47.2 2.2 %multiply_reduce_fusion.1 = f32[1024]{0:T(1024)S(1)} fusion(bf16[1024,1024]{1,0:T(8,128)(2,1)} %all-gather.5.cloned.1.call-done), kind=kLoop, calls=%fused_computation.3 | loop fusion | flops 3144704 | bytes 2101248 | tf_op jit(solution)/shard_map/reduce_sum | solution.py:10
  49.5 46.6 %all-gather.3.cloned.1.call-done = bf16[2048,1024]{1,0:T(8,128)(2,1)} async-done(((bf16[256,1024]{1,0:T(8,128)(2,1)}), bf16[2048,1024]{1,0:T(8,128)(2,1)}) %all-gather.3.cloned.1.call-update) | async-done | bytes 4194320 | tf_op jit(solution)/shard_map/all_gather | solution.py:29
  96.0 3.1 %multiply_reduce_fusion = f32[2048]{0:T(1024)S(1)} fusion(bf16[2048,1024]{1,0:T(8,128)(2,1)} %all-gather.3.cloned.1.call-done), kind=kLoop, calls=%fused_computation.2 | loop fusion | flops 6289408 | bytes 4202496 | tf_op jit(solution)/shard_map/reduce_sum | solution.py:10
  99.1 0.0 copy-done
  99.1 9.4 %fusion.1 = f32[2048,256]{1,0:T(8,128)} fusion(bf16[1024,256]{1,0:T(8,128)(2,1)S(1)} %all_gather.11, f32[1024]{0:T(1024)S(1)} %multiply_reduce_fusion.1, f32[2048]{0:T(1024)S(1)} %multiply_reduce_fusion, bf16[2048,1024]{1,0:T(8,128)(2,1)} %all-gather.3.cloned.1.call-done, bf16[1024,1024]{1,0:T(8,128)(2,1)S(1)} %copy-done), kind=kOutput, calls=%fused_computation.4 | convolution fusion | flops 5377097728 | bytes 8925184 | tf_op jit(solution)/shard_map/dot_general | solution.py:31
  108.5 0.0 reduce-scatter.2.cloned.1.call-update
  108.5 34.8 %reduce-scatter.2.cloned.1.call-done = f32[256,256]{1,0:T(8,128)} async-done(((f32[2048,256]{1,0:T(8,128)}), f32[256,256]{1,0:T(8,128)}) %reduce-scatter.2.cloned.1.call-update) | async-done | bytes 262160 | tf_op jit(solution)/shard_map/reduce_scatter | solution.py:32
  143.3 1.7 %broadcast_multiply_fusion = f32[256,256]{1,0:T(8,128)} fusion(f32[256,256]{1,0:T(8,128)} %reduce-scatter.2.cloned.1.call-done), kind=kLoop, calls=%fused_computation.5 | loop fusion | flops 65536 | bytes 524288 | tf_op jit(solution)/shard_map/mul | solution.py:33
Async XLA Ops:
  6.5 40.7 %all-gather.5.cloned.1.call-start = ((), (), s32[]{:S(2)}) async-start(), calls=%async_computation.2 | async-start | bytes 2621440 | tf_op jit(solution)/shard_map/all_gather | solution.py:25
  7.3 88.8 %all-gather.3.cloned.1.call-start = ((), (), s32[]{:S(2)}) async-start(), calls=%async_computation.1 | async-start | bytes 4718592 | tf_op jit(solution)/shard_map/all_gather | solution.py:29
  8.0 135.3 %reduce-scatter.2.cloned.1.call-start = ((), (), s32[]{:S(2)}) async-start(), calls=%async_computation.3 | async-start | bytes 2359296 | tf_op jit(solution)/shard_map/reduce_scatter | solution.py:32
  47.2 51.9 %copy-start = (bf16[1024,1024]{1,0:T(8,128)(2,1)S(1)}, bf16[1024,1024]{1,0:T(8,128)(2,1)}, u32[]{:S(2)}) copy-start(bf16[1024,1024]{1,0:T(8,128)(2,1)} %all-gather.5.cloned.1.call-done) | copy-start | bytes 6291460
Sparse Core Ops, SparseCore 0:
  9.2 38.0 all-gather.4
  48.8 47.1 all-gather.2
  108.7 34.5 reduce-scatter.1
where the time goes:
time: 152 us; the launch traced here: 151 us
  waiting for transfers between devices  110 us (72%)
  between operations  13.1 us (9%)
  blocking collectives  11.8 us (8%)
  matrix products  9.4 us (6%)
  other arithmetic  6.96 us (5%)
    all_gather x1, waiting for transfers between devices, per_device(): shard_rows = lax.all_gather(fingerprints, 'col', axis=0, tiled=True)  46.6 us
    reduce_scatter x1, waiting for transfers between devices, per_device(): lax.psum_scatter(partial_value, 'col', scatter_dimension=0, tiled=True)  34.8 us
    all_gather x1, waiting for transfers between devices, per_device(): lax.all_gather(fingerprints, 'row', axis=0, tiled=True)  27.4 us
    all_gather x1, blocking collectives, per_device(): lax.all_gather(probes, 'row', axis=0, tiled=True)  11.8 us
    dot_general x1, matrix products, per_device(): jnp.dot(kernel, column_probes, preferred_element_type=jnp.float32)  9.4 us
    reduce_sum x2, other arithmetic, squares(): return jnp.sum(values * values, axis=1)  5.29 us
  transfers between devices with their start and end apart: 3, of which 3 were waited for; matrix products, arithmetic and copies ran while one was open for 1% of the time, Pallas kernels for 0%

commit v1 on v0

--- a/solution.py
+++ b/solution.py
@@ -1,8 +1,33 @@
+import functools
 import math
 import jax
 import jax.numpy as jnp
 from jax import lax
 from jax.sharding import PartitionSpec as P
+from jax.lax import axis_index, axis_size, ppermute
+
+
+def note_domain_on_mesh(patch, in_dim):
+    val, vec_out, extra = (axis_size("col"), axis_index("col"), patch.shape[in_dim])
+    grid = [h * val if dd == in_dim else h for dd, h in enumerate(patch.shape)]
+    x_now = lax.dynamic_update_slice_in_dim(
+        jnp.zeros(grid, patch.dtype), patch, vec_out * extra, axis=in_dim
+    )
+    high = g_now = patch
+    for j0 in range(1, val // 2 + 1):
+        high = ppermute(high, "col", [(dd, (dd + 1) % val) for dd in range(val)])
+        x_now = lax.dynamic_update_slice_in_dim(
+            x_now, high, (vec_out - j0) % val * extra, axis=in_dim
+        )
+        if 2 * j0 < val:
+            g_now = ppermute(g_now, "col", [(dd, (dd - 1) % val) for dd in range(val)])
+            x_now = lax.dynamic_update_slice_in_dim(
+                x_now, g_now, (vec_out + j0) % val * extra, axis=in_dim
+            )
+    return x_now
+
+
+patches_form = functools.partial(note_domain_on_mesh, in_dim=0)
 
 
 def squares(rows_now):
@@ -26,7 +51,7 @@
         lax.all_gather(probes, "row", axis=0, tiled=True),
     )
     column_sq = squares(column_rows)
-    shard_rows = lax.all_gather(fingerprints, "col", axis=0, tiled=True)
+    shard_rows = patches_form(fingerprints)
     kernel = tanimoto(shard_rows, column_rows, squares(shard_rows), column_sq)
     partial_value = jnp.dot(kernel, column_probes, preferred_element_type=jnp.float32)
     owned = lax.psum_scatter(partial_value, "col", scatter_dimension=0, tiled=True)

time: 152 us -> 126 us (0.83)
  waiting for transfers between devices: 110 us -> 67.2 us
  starting transfers between devices: 0.08 us -> 10.9 us
  blocking collectives: 11.8 us -> 16.8 us
  local copies, waits for them, and re-layouts: 0.01 us -> 2.81 us
  other arithmetic: 6.96 us -> 4.63 us
    all_gather x1 -> x0, waiting for transfers between devices: 46.6 us -> none  [per_device(): shard_rows = lax.all_gather(fingerprints, 'col', axis=0, tiled=True)]
    ppermute x0 -> x7, waiting for transfers between devices: none -> 32.2 us  [the longest x4 21.4 us: note_domain_on_mesh(): high = ppermute(high, 'col', [(dd, (dd + 1) % val) for dd in range(val)])]
    all_gather x1, waiting for transfers between devices: 27.4 us -> 0.02 us  [per_device(): lax.all_gather(fingerprints, 'row', axis=0, tiled=True)]
    ppermute x0 -> x7, starting transfers between devices: none -> 10.8 us  [the longest x3 10.3 us: note_domain_on_mesh(): g_now = ppermute(g_now, 'col', [(dd, (dd - 1) % val) for dd in range(val)])]
    all_gather x1, blocking collectives: 11.8 us -> 16.8 us  [per_device(): lax.all_gather(probes, 'row', axis=0, tiled=True)]
    reduce_sum x2, other arithmetic: 5.29 us -> 2.95 us  [squares(): return jnp.sum(values * values, axis=1)]
    unnamed x2 -> x8, local copies, waits for them, and re-layouts: 0.01 us -> 1.94 us
  transfers between devices with their start and end apart: 3 -> 9, of which waited for: 3 -> 6; matrix products, arithmetic and copies ran while one was open for 1% -> 1% of each run, Pallas kernels for 0% -> 0%
where the time goes in v1:
time: 126 us
  waiting for transfers between devices  67.2 us (53%)
  blocking collectives  16.8 us (13%)
  between operations  13.5 us (11%)
  starting transfers between devices  10.9 us (9%)
  matrix products  10.1 us (8%)
  other arithmetic  4.63 us (4%)
  local copies, waits for them, and re-layouts  2.81 us (2%)
    reduce_scatter x1, waiting for transfers between devices, per_device(): lax.psum_scatter(partial_value, 'col', scatter_dimension=0, tiled=True)  34.2 us
    ppermute x4, waiting for transfers between devices, note_domain_on_mesh(): high = ppermute(high, 'col', [(dd, (dd + 1) % val) for dd in range(val)])  21.4 us
    all_gather x1, blocking collectives, per_device(): lax.all_gather(probes, 'row', axis=0, tiled=True)  16.8 us
    ppermute x3, waiting for transfers between devices, note_domain_on_mesh(): g_now = ppermute(g_now, 'col', [(dd, (dd - 1) % val) for dd in range(val)])  10.8 us
    ppermute x3, starting transfers between devices, note_domain_on_mesh(): g_now = ppermute(g_now, 'col', [(dd, (dd - 1) % val) for dd in range(val)])  10.3 us
    dot_general x1, matrix products, per_device(): jnp.dot(kernel, column_probes, preferred_element_type=jnp.float32)  10.1 us
    reduce_sum x2, other arithmetic, squares(): return jnp.sum(values * values, axis=1)  2.95 us
  transfers between devices with their start and end apart: 9, of which 6 were waited for; matrix products, arithmetic and copies ran while one was open for 1% of the time, Pallas kernels for 0%

profile of v1, /device:TPU:0, one launch (start us, length us, event | category | flops | bytes accessed | tf_op | source)
XLA Modules:
  0.0 125.9 jit_solution(15668860072813294225)
XLA Ops:
  6.5 0.0 copy-start.1
  6.5 0.0 all-gather.2.cloned.1.call-start
  6.5 0.7 all-gather.2.cloned.1.call-update
  7.3 0.0 reduce-scatter.2.cloned.1.call-start
  7.3 0.5 collective-permute-start
  7.8 4.1 %collective-permute-start.1 = (bf16[256,1024]{1,0:T(8,128)(2,1)}, bf16[256,1024]{1,0:T(8,128)(2,1)S(1)}, u32[]{:S(2)}, u32[]{:S(2)}) collective-permute-start(bf16[256,1024]{1,0:T(8,128)(2,1)} %param.2), channel_id=1, source_target_pairs={{0,7},{1,0},{2,1},{3,2},{4,3},{5,4},{6,5},{7,6},{8,15},{9,8},{10,9... | collective-permute-start | bytes 1572872 | tf_op jit(solution)/shard_map/ppermute | solution.py:23
  11.9 10.0 %collective-permute-done = bf16[256,1024]{1,0:T(8,128)(2,1)S(1)} collective-permute-done((bf16[256,1024]{1,0:T(8,128)(2,1)}, bf16[256,1024]{1,0:T(8,128)(2,1)S(1)}, u32[]{:S(2)}, u32[]{:S(2)}) %collective-permute-start) | collective-permute-done | bytes 524320 | tf_op jit(solution)/shard_map/ppermute | solution.py:18
  21.9 0.0 collective-permute-start.2
  21.9 0.6 collective-permute-done.1
  22.5 3.7 %collective-permute-start.3 = (bf16[256,1024]{1,0:T(8,128)(2,1)S(1)}, bf16[256,1024]{1,0:T(8,128)(2,1)S(1)}, u32[]{:S(2)}, u32[]{:S(2)}) collective-permute-start(bf16[256,1024]{1,0:T(8,128)(2,1)S(1)} %collective-permute-done.1), channel_id=1, source_target_pairs={{0,7},{1,0},{2,1},{3,2},{4,3},{5,4},{6,5},{7,6},{8,15},{9,8},{10,9... | collective-permute-start | bytes 1572872 | tf_op jit(solution)/shard_map/ppermute | solution.py:23
  26.2 8.2 %collective-permute-done.2 = bf16[256,1024]{1,0:T(8,128)(2,1)S(1)} collective-permute-done((bf16[256,1024]{1,0:T(8,128)(2,1)S(1)}, bf16[256,1024]{1,0:T(8,128)(2,1)S(1)}, u32[]{:S(2)}, u32[]{:S(2)}) %collective-permute-start.2) | collective-permute-done | bytes 524320 | tf_op jit(solution)/shard_map/ppermute | solution.py:18
  34.4 0.0 collective-permute-start.4
  34.4 0.0 copy-done.2
  34.4 16.8 %all_gather.7 = bf16[1024,256]{1,0:T(8,128)(2,1)S(1)} all-gather(bf16[256,256]{1,0:T(8,128)(2,1)} %param.3), channel_id=1, replica_groups=mesh['row'=4,'col'=8] {'row'}, dimensions={0}, use_global_device_ids=true | all-gather | bytes 655360 | tf_op jit(solution)/shard_map/all_gather | solution.py:51
  51.1 0.5 broadcast_in_dim.2
  51.7 0.0 copy-done.1
  51.7 0.0 collective-permute-done.3
  51.7 2.5 %collective-permute-start.5 = (bf16[256,1024]{1,0:T(8,128)(2,1)S(1)}, bf16[256,1024]{1,0:T(8,128)(2,1)S(1)}, u32[]{:S(2)}, u32[]{:S(2)}) collective-permute-start(bf16[256,1024]{1,0:T(8,128)(2,1)S(1)} %collective-permute-done.3), channel_id=1, source_target_pairs={{0,7},{1,0},{2,1},{3,2},{4,3},{5,4},{6,5},{7,6},{8,15},{9,8},{10,9... | collective-permute-start | bytes 1572872 | tf_op jit(solution)/shard_map/ppermute | solution.py:23
  54.2 0.0 copy-done.3
  54.2 0.0 collective-permute-done.4
  54.3 0.1 collective-permute-start.6
  54.5 10.2 %collective-permute-done.5 = bf16[256,1024]{1,0:T(8,128)(2,1)S(1)} collective-permute-done((bf16[256,1024]{1,0:T(8,128)(2,1)S(1)}, bf16[256,1024]{1,0:T(8,128)(2,1)S(1)}, u32[]{:S(2)}, u32[]{:S(2)}) %collective-permute-start.5) | collective-permute-done | bytes 524320 | tf_op jit(solution)/shard_map/ppermute | solution.py:23
  64.8 3.3 %collective-permute-done.6 = bf16[256,1024]{1,0:T(8,128)(2,1)S(1)} collective-permute-done((bf16[256,1024]{1,0:T(8,128)(2,1)S(1)}, bf16[256,1024]{1,0:T(8,128)(2,1)S(1)}, u32[]{:S(2)}, u32[]{:S(2)}) %collective-permute-start.6) | collective-permute-done | bytes 524320 | tf_op jit(solution)/shard_map/ppermute | solution.py:18
  68.1 0.0 copy-start
  68.1 1.9 %copy-done = bf16[2048,1024]{1,0:T(8,128)(2,1)} copy-done((bf16[2048,1024]{1,0:T(8,128)(2,1)}, bf16[2048,1024]{1,0:T(8,128)(2,1)S(1)}, u32[]{:S(2)}) %copy-start) | copy-done | bytes 4194328
  70.1 0.9 multiply_reduce_fusion
  70.9 0.0 all-gather.2.cloned.1.call-done
  71.0 2.1 %multiply_reduce_fusion.1 = f32[1024]{0:T(1024)S(1)} fusion(bf16[1024,1024]{1,0:T(8,128)(2,1)} %all-gather.2.cloned.1.call-done), kind=kLoop, calls=%fused_computation.3 | loop fusion | flops 3144704 | bytes 2101248 | tf_op jit(solution)/shard_map/reduce_sum | solution.py:35
  73.0 10.1 %fusion.1 = f32[2048,256]{1,0:T(8,128)} fusion(bf16[1024,256]{1,0:T(8,128)(2,1)S(1)} %all_gather.7, f32[1024]{0:T(1024)S(1)} %multiply_reduce_fusion.1, f32[2048]{0:T(1024)S(1)} %multiply_reduce_fusion, bf16[2048,1024]{1,0:T(8,128)(2,1)} %copy-done, bf16[1024,1024]{1,0:T(8,128)(2,1)} %all-gather.2.cloned.1.call-done), kind=kOutput, calls=%fused_computation.4 | convolution fusion | flops 5377097728 | bytes 8925184 | tf_op jit(solution)/shard_map/dot_general | solution.py:56
  83.2 0.0 reduce-scatter.2.cloned.1.call-update
  83.2 34.2 %reduce-scatter.2.cloned.1.call-done = f32[256,256]{1,0:T(8,128)} async-done(((f32[2048,256]{1,0:T(8,128)}), f32[256,256]{1,0:T(8,128)}) %reduce-scatter.2.cloned.1.call-update) | async-done | bytes 262160 | tf_op jit(solution)/shard_map/reduce_scatter | solution.py:57
  117.4 1.7 %broadcast_multiply_fusion = f32[256,256]{1,0:T(8,128)} fusion(f32[256,256]{1,0:T(8,128)} %reduce-scatter.2.cloned.1.call-done), kind=kLoop, calls=%fused_computation.5 | loop fusion | flops 65536 | bytes 524288 | tf_op jit(solution)/shard_map/mul | solution.py:58
  (10 shorter events, 0.4 us)
Async XLA Ops:
  6.5 45.1 %copy-start.1 = (bf16[256,1024]{1,0:T(8,128)(2,1)S(1)}, bf16[256,1024]{1,0:T(8,128)(2,1)}, u32[]{:S(2)}) copy-start(bf16[256,1024]{1,0:T(8,128)(2,1)} %param.2) | copy-start | bytes 1572868
  6.5 64.4 %all-gather.2.cloned.1.call-start = ((), (), s32[]{:S(2)}) async-start(), calls=%async_computation.1 | async-start | bytes 2621440 | tf_op jit(solution)/shard_map/all_gather | solution.py:50
  7.3 110.1 %reduce-scatter.2.cloned.1.call-start = ((), (), s32[]{:S(2)}) async-start(), calls=%async_computation.2 | async-start | bytes 2359296 | tf_op jit(solution)/shard_map/reduce_scatter | solution.py:57
  7.3 14.6 %collective-permute-start = (bf16[256,1024]{1,0:T(8,128)(2,1)}, bf16[256,1024]{1,0:T(8,128)(2,1)S(1)}, u32[]{:S(2)}, u32[]{:S(2)}) collective-permute-start(bf16[256,1024]{1,0:T(8,128)(2,1)} %param.2), channel_id=1, source_target_pairs={{0,1},{1,2},{2,3},{3,4},{4,5},{5,6},{6,7},{7,0},{8,9},{9,10},{10,1... | collective-permute-start | bytes 1572872 | tf_op jit(solution)/shard_map/ppermute | solution.py:18
  7.8 14.7 %collective-permute-start.1 = (bf16[256,1024]{1,0:T(8,128)(2,1)}, bf16[256,1024]{1,0:T(8,128)(2,1)S(1)}, u32[]{:S(2)}, u32[]{:S(2)}) collective-permute-start(bf16[256,1024]{1,0:T(8,128)(2,1)} %param.2), channel_id=1, source_target_pairs={{0,7},{1,0},{2,1},{3,2},{4,3},{5,4},{6,5},{7,6},{8,15},{9,8},{10,9... | collective-permute-start | bytes 1572872 | tf_op jit(solution)/shard_map/ppermute | solution.py:23
  21.9 12.5 %copy-start.2 = (bf16[256,1024]{1,0:T(8,128)(2,1)}, bf16[256,1024]{1,0:T(8,128)(2,1)S(1)}, u32[]{:S(2)}) copy-start(bf16[256,1024]{1,0:T(8,128)(2,1)S(1)} %collective-permute-done) | copy-start | bytes 1572868
  21.9 12.5 %collective-permute-start.2 = (bf16[256,1024]{1,0:T(8,128)(2,1)S(1)}, bf16[256,1024]{1,0:T(8,128)(2,1)S(1)}, u32[]{:S(2)}, u32[]{:S(2)}) collective-permute-start(bf16[256,1024]{1,0:T(8,128)(2,1)S(1)} %collective-permute-done), channel_id=1, source_target_pairs={{0,1},{1,2},{2,3},{3,4},{4,5},{5,6},{6,7},{7,0},{8,9},{9,10},{10,1... | collective-permute-start | bytes 1572872 | tf_op jit(solution)/shard_map/ppermute | solution.py:18
  22.5 29.2 %collective-permute-start.3 = (bf16[256,1024]{1,0:T(8,128)(2,1)S(1)}, bf16[256,1024]{1,0:T(8,128)(2,1)S(1)}, u32[]{:S(2)}, u32[]{:S(2)}) collective-permute-start(bf16[256,1024]{1,0:T(8,128)(2,1)S(1)} %collective-permute-done.1), channel_id=1, source_target_pairs={{0,7},{1,0},{2,1},{3,2},{4,3},{5,4},{6,5},{7,6},{8,15},{9,8},{10,9... | collective-permute-start | bytes 1572872 | tf_op jit(solution)/shard_map/ppermute | solution.py:23
  34.4 19.9 %collective-permute-start.4 = (bf16[256,1024]{1,0:T(8,128)(2,1)S(1)}, bf16[256,1024]{1,0:T(8,128)(2,1)S(1)}, u32[]{:S(2)}, u32[]{:S(2)}) collective-permute-start(bf16[256,1024]{1,0:T(8,128)(2,1)S(1)} %collective-permute-done.2), channel_id=1, source_target_pairs={{0,1},{1,2},{2,3},{3,4},{4,5},{5,6},{6,7},{7,0},{8,9},{9,10},{10,1... | collective-permute-start | bytes 1572872 | tf_op jit(solution)/shard_map/ppermute | solution.py:18
  34.4 19.8 %copy-start.3 = (bf16[256,1024]{1,0:T(8,128)(2,1)S(1)}, bf16[256,1024]{1,0:T(8,128)(2,1)}, u32[]{:S(2)}) copy-start(bf16[256,1024]{1,0:T(8,128)(2,1)} %copy-done.2) | copy-start | bytes 1572868
  51.7 13.0 %collective-permute-start.5 = (bf16[256,1024]{1,0:T(8,128)(2,1)S(1)}, bf16[256,1024]{1,0:T(8,128)(2,1)S(1)}, u32[]{:S(2)}, u32[]{:S(2)}) collective-permute-start(bf16[256,1024]{1,0:T(8,128)(2,1)S(1)} %collective-permute-done.3), channel_id=1, source_target_pairs={{0,7},{1,0},{2,1},{3,2},{4,3},{5,4},{6,5},{7,6},{8,15},{9,8},{10,9... | collective-permute-start | bytes 1572872 | tf_op jit(solution)/shard_map/ppermute | solution.py:23
  54.3 13.8 %collective-permute-start.6 = (bf16[256,1024]{1,0:T(8,128)(2,1)S(1)}, bf16[256,1024]{1,0:T(8,128)(2,1)S(1)}, u32[]{:S(2)}, u32[]{:S(2)}) collective-permute-start(bf16[256,1024]{1,0:T(8,128)(2,1)S(1)} %collective-permute-done.4), channel_id=1, source_target_pairs={{0,1},{1,2},{2,3},{3,4},{4,5},{5,6},{6,7},{7,0},{8,9},{9,10},{10,1... | collective-permute-start | bytes 1572872 | tf_op jit(solution)/shard_map/ppermute | solution.py:18
  68.1 1.9 %copy-start = (bf16[2048,1024]{1,0:T(8,128)(2,1)}, bf16[2048,1024]{1,0:T(8,128)(2,1)S(1)}, u32[]{:S(2)}) copy-start(bf16[2048,1024]{1,0:T(8,128)(2,1)S(1)} %constant_dynamic-update-slice_fusion) | copy-start | bytes 12582916
Sparse Core Ops, SparseCore 0:
  9.2 42.0 all-gather.1
  83.3 34.0 reduce-scatter.1
